TPU v7x, 128 devices: a whole 4x4x4 slice. The times are simulated.
128 devices in a mesh: src: 16 (over y_lo, z, core), snk: 8 (over x, y_hi).
Axes of the slice: x: 4, y: 4 (y_hi: 2, y_lo: 2; y = y_hi * 2 + y_lo), z: 4, core: 2. Of those that a mesh axis runs over, the one named last changes fastest.
Arguments:
- perambulators: bfloat16 [16, 16, 2, 512, 512], P('src'), may hold values from -2 to 2, as said below
- elements: bfloat16 [16, 8, 2, 512, 512], P('src', None, None, 'snk'), may hold values from -0.25 to 0.25
Outputs:
- correlator: float32 [2, 16, 16, 8, 8], P(None, 'src', 'snk')
Inputs may be any that keep to these rules, and one draw needn't show every extreme that they name: For all times x, y: perambulators[x, y] = Q(y<-x), i.e.
All inputs are finite; a program needn't handle non-finite values.
Results may differ from a plain program's by a relative error of at most 0.0041.
Values may be sent and summed in bfloat16 or wider, within the bound.
A program may use at most 128 MiB of HBM per device.

v0:
```python
import jax
import jax.numpy as jnp
from jax import lax
from jax.experimental import pallas as pl
from jax.experimental.pallas import tpu as pltpu
from jax.sharding import PartitionSpec as P

MESH = pl.DeviceIdType.MESH
UNITS = 9
NT_DIMS = (((1,), (1,)), ((), ()))

FLIP, NEXT, FLIP_PREV, HALF = 0, 1, 2, 3
SIB_OWN, SIB_FLIP, SIB_NEXT, SIB_FLIP_PREV, SIB_HALF = 4, 5, 6, 7, 8


def dot(a, b):
    return jnp.dot(a, b, preferred_element_type=jnp.float32)


def dot_nt(a, b):
    return lax.dot_general(a, b, NT_DIMS, preferred_element_type=jnp.float32)


def exact_nt(a, b):
    return lax.dot_general(
        a, b, NT_DIMS, preferred_element_type=jnp.float32, precision=lax.Precision.HIGHEST
    )


def kernel(
    peram, elem, out, full, other, mats, left, xs, ys, parts, sums, swapped,
    load_sem, send_sem, recv_sem, part_send, part_recv, swap_send, swap_recv,
):
    src = lax.axis_index("src")
    snk = lax.axis_index("snk")
    core = lax.rem(src, 2)
    z = lax.rem(src // 2, 4)
    ylo = src // 8
    x = snk // 2
    yhi = lax.rem(snk, 2)
    y = yhi * 2 + ylo
    tau = src // 2
    ops = elem.shape[1]
    rows = elem.shape[3]

    def place(px, py, pz, pc):
        return ((lax.rem(py, 2) * 4 + pz) * 2 + pc, px * 2 + py // 2)

    xr = lax.rem(x + 1, 4)
    xl = lax.rem(x + 3, 4)
    xo = lax.rem(x + 2, 4)
    yn = lax.rem(y + 1, 4)
    yp = lax.rem(y + 3, 4)
    yo = lax.rem(y + 2, 4)
    zn = lax.rem(z + 1, 4)
    zp = lax.rem(z + 3, 4)
    zo = lax.rem(z + 2, 4)
    yoh = yo // 2
    dev_xr = place(xr, y, z, core)
    dev_xl = place(xl, y, z, core)
    dev_yo = place(x, yo, z, core)
    y_to = lax.rem(y + 3 + 2 * core, 4)
    y_from = lax.rem(y + 1 + 2 * core, 4)
    y_from_sib = lax.rem(y + 3 + 2 * core, 4)
    dev_flip = place(x, y_to, z, core)
    dev_flip_back = place(x, y_from, z, core)
    dev_zn = place(x, y, zn, core)
    dev_zp = place(x, y, zp, core)
    dev_zo = place(x, y, zo, core)
    dev_sib = (src + 1 - 2 * core, snk)

    own_rows = snk
    flip_rows = x * 2 + y_from // 2
    flip_rows_sib = x * 2 + y_from_sib // 2
    low = z < 2
    flip_tau = (1 - ylo) * 4 + z
    next_tau = ylo * 4 + zn
    prev_tau = (1 - ylo) * 4 + zp
    half_tau = jnp.where(low, ylo, 1 - ylo) * 4 + zo
    sib = 1 - core
    flip_core = lax.rem(core + ylo, 2)
    taus = [tau, tau, flip_tau, next_tau, next_tau, prev_tau, prev_tau, half_tau, half_tau]
    cores = [core, sib, flip_core, core, sib, core, sib, core, sib]
    blocks = [
        own_rows,
        own_rows,
        jnp.where(ylo == 0, flip_rows, flip_rows_sib),
        own_rows,
        own_rows,
        flip_rows,
        flip_rows_sib,
        jnp.where(low, own_rows, flip_rows),
        jnp.where(low, own_rows, flip_rows_sib),
    ]
    slots = [
        None, SIB_OWN, jnp.where(ylo == 0, FLIP, SIB_FLIP), NEXT, SIB_NEXT,
        FLIP_PREV, SIB_FLIP_PREV, HALF, SIB_HALF,
    ]

    own_slice = full.at[:, :, pl.ds(pl.multiple_of(snk * rows, rows), rows), :]
    own_load = pltpu.make_async_copy(elem.at[0], own_slice, load_sem.at[UNITS])
    own_load.start()
    loads = []
    for u in range(UNITS):
        load = pltpu.make_async_copy(
            peram.at[0, taus[u] * 2 + cores[u]], mats.at[u], load_sem.at[u]
        )
        load.start()
        loads.append(load)

    swapped[...] = jnp.zeros_like(swapped)

    barrier = pltpu.get_barrier_semaphore()
    for step in range(1, 8):
        pl.semaphore_signal(
            barrier, inc=1, device_id=(src, lax.rem(snk + step, 8)), device_id_type=MESH
        )
    for target in (dev_flip, dev_flip_back, dev_zn, dev_zp, dev_zo, dev_sib):
        pl.semaphore_signal(barrier, inc=1, device_id=target, device_id_type=MESH)
    outside = snk != tau

    @pl.when(outside)
    def _():
        for c in range(2):
            pl.semaphore_signal(barrier, inc=1, device_id=(snk * 2 + c, tau), device_id_type=MESH)

    pl.semaphore_wait(barrier, jnp.where(outside, 15, 13))

    sent = []
    counter = [0]

    def remote(source, target, device):
        k = counter[0]
        counter[0] += 1
        copy = pltpu.make_async_remote_copy(
            src_ref=source, dst_ref=target, send_sem=send_sem.at[k], recv_sem=recv_sem.at[k],
            device_id=device, device_id_type=MESH,
        )
        copy.start()
        sent.append(copy)
        return k

    def arrived(k, target):
        pltpu.make_async_remote_copy(
            src_ref=target, dst_ref=target, send_sem=send_sem.at[k], recv_sem=recv_sem.at[k],
            device_id=dev_sib, device_id_type=MESH,
        ).wait_recv()

    def rows_of(px, pyh, first=0, count=ops):
        start = pl.multiple_of((px * 2 + pyh) * rows, rows)
        return full.at[pl.ds(first, count), :, pl.ds(start, rows), :]

    mine = elem.at[0]
    half = ops // 2
    k_flip = remote(mine, other.at[FLIP], dev_flip)
    k_xr = remote(mine, rows_of(x, yhi), dev_xr)
    k_xl = remote(mine, rows_of(x, yhi), dev_xl)
    k_yo = remote(mine, rows_of(x, yhi), dev_yo)
    k_next = remote(mine, other.at[NEXT], dev_zp)
    k_sib = remote(mine, other.at[SIB_OWN], dev_sib)

    col = lax.broadcasted_iota(jnp.int32, (rows, 512), 1)
    lane_sign = jnp.where(col < 256, 1.0, -1.0) * jnp.where(x < 2, 1.0, -1.0)

    def prepare(u):
        loads[u].wait()
        start = pl.multiple_of(blocks[u] * rows, rows)
        re = mats[u, 0, pl.ds(start, rows), :].astype(jnp.float32) * lane_sign
        im = mats[u, 1, pl.ds(start, rows), :].astype(jnp.float32) * lane_sign
        left[0, u, 0] = re.astype(jnp.bfloat16)
        left[0, u, 1] = (-im).astype(jnp.bfloat16)
        left[1, u, 0] = im.astype(jnp.bfloat16)
        left[1, u, 1] = re.astype(jnp.bfloat16)

    def sink_product(u):
        prepare(u)

        def tile(n, carry):
            cols = pl.ds(pl.multiple_of(n * 256, 256), 256)
            if u == 0:
                start = pl.multiple_of(snk * rows, rows)
                er = full[:, 0, pl.ds(start, rows), :]
                ei = full[:, 1, pl.ds(start, rows), :]
            else:
                er = other[slots[u], :, 0]
                ei = other[slots[u], :, 1]
            er = er.reshape(ops * rows, 512)
            ei = ei.reshape(ops * rows, 512)
            pr = mats[u, 0, :, cols]
            pi = mats[u, 1, :, cols]
            re = dot(er, pr) - dot(ei, pi)
            im = dot(er, pi) + dot(ei, pr)
            xs[u, 0, :, :, cols] = re.astype(jnp.bfloat16).reshape(ops, rows, 256)
            xs[u, 1, :, :, cols] = im.astype(jnp.bfloat16).reshape(ops, rows, 256)
            return carry

        lax.fori_loop(0, 2, tile, 0)

    def source_product(px):
        cols = pl.ds(pl.multiple_of(px * 128, 128), 128)

        def tile(q, carry):
            o = q * 2
            wr = full[pl.ds(o, 2), 0, cols, :].reshape(256, 512)
            wi = full[pl.ds(o, 2), 1, cols, :].reshape(256, 512)
            for m in range(3):
                a = left[0, 3 * m : 3 * m + 3].reshape(384, 512)
                b = left[1, 3 * m : 3 * m + 3].reshape(384, 512)
                r = (dot_nt(a, wr) + dot_nt(b, wi)).astype(jnp.bfloat16)
                ys[3 * m : 3 * m + 3, :, o, :, cols] = r[:, :128].reshape(3, 2, rows, 128)
                ys[3 * m : 3 * m + 3, :, o + 1, :, cols] = r[:, 128:].reshape(3, 2, rows, 128)
            return carry

        lax.fori_loop(0, ops // 2, tile, 0)

    own_load.wait()
    sink_product(0)
    arrived(k_flip, other.at[FLIP])
    k_prev = remote(other.at[FLIP], other.at[FLIP_PREV], dev_zn)
    k_half = counter[0]
    counter[0] += 1

    def half_copy(source):
        return pltpu.make_async_remote_copy(
            src_ref=source, dst_ref=other.at[HALF], send_sem=send_sem.at[k_half],
            recv_sem=recv_sem.at[k_half], device_id=dev_zo, device_id_type=MESH,
        )

    @pl.when(low)
    def _():
        half_copy(other.at[FLIP]).start()

    @pl.when(jnp.logical_not(low))
    def _():
        half_copy(mine).start()

    k_sib_flip = remote(other.at[FLIP], other.at[SIB_FLIP], dev_sib)
    arrived(k_sib, other.at[SIB_OWN])
    sink_product(1)
    arrived(k_sib_flip, other.at[SIB_FLIP])
    sink_product(2)

    def forward(k_from_left, k_from_right, pyh):
        arrived(k_from_left, rows_of(xl, pyh))
        on_right = remote(rows_of(xl, pyh, half, half), rows_of(xl, pyh, half, half), dev_xr)
        arrived(k_from_right, rows_of(xr, pyh))
        on_left = remote(rows_of(xr, pyh, 0, half), rows_of(xr, pyh, 0, half), dev_xl)
        return on_right, on_left

    own_right, own_left = forward(k_xr, k_xl, yhi)
    arrived(k_yo, rows_of(x, yoh))
    k_oxr = remote(rows_of(x, yoh), rows_of(x, yoh), dev_xr)
    k_oxl = remote(rows_of(x, yoh), rows_of(x, yoh), dev_xl)
    arrived(k_next, other.at[NEXT])
    k_sib_next = remote(other.at[NEXT], other.at[SIB_NEXT], dev_sib)
    sink_product(3)
    arrived(k_sib_next, other.at[SIB_NEXT])
    sink_product(4)
    arrived(k_prev, other.at[FLIP_PREV])
    k_sib_prev = remote(other.at[FLIP_PREV], other.at[SIB_FLIP_PREV], dev_sib)
    sink_product(5)
    arrived(k_sib_prev, other.at[SIB_FLIP_PREV])
    sink_product(6)
    arrived(k_half, other.at[HALF])
    k_sib_half = remote(other.at[HALF], other.at[SIB_HALF], dev_sib)
    sink_product(7)
    arrived(k_sib_half, other.at[SIB_HALF])
    sink_product(8)
    source_product(x)
    other_right, other_left = forward(k_oxr, k_oxl, yoh)
    source_product(xl)
    source_product(xr)
    for k_right, k_left, pyh in ((own_right, own_left, yhi), (other_right, other_left, yoh)):
        arrived(k_right, rows_of(xo, pyh, half, half))
        arrived(k_left, rows_of(xo, pyh, 0, half))
    source_product(xo)

    parts[...] = jnp.zeros_like(parts)
    r_iota = lax.broadcasted_iota(jnp.int32, (256, 256), 0)
    c_iota = lax.broadcasted_iota(jnp.int32, (256, 256), 1)
    same = lax.rem(r_iota, 16) == lax.rem(c_iota, 16)
    pick_row = lax.broadcasted_iota(jnp.int32, (16, 256), 0)
    pick_group = lax.broadcasted_iota(jnp.int32, (16, 256), 1) // 16
    straight = jnp.where(pick_row == pick_group, 1.0, 0.0)
    crossed = jnp.where(
        pick_row < 8,
        jnp.where(pick_group == pick_row + 8, -1.0, 0.0),
        jnp.where(pick_group == pick_row - 8, 1.0, 0.0),
    )

    def trace(u):
        total = jnp.zeros((256, 256), jnp.float32)
        for s in range(rows // 16):
            a = xs[u, :, :, 16 * s : 16 * s + 16, :].reshape(256, 512)
            b = ys[u, :, :, 16 * s : 16 * s + 16, :].reshape(256, 512)
            total += dot_nt(a, b)
        total = jnp.where(same, total, 0.0)
        rowed = jnp.sum(total.reshape(16, 16, 256), axis=1)
        re_rows = rowed[0:8]
        im_rows = rowed[8:16]
        plain = exact_nt(re_rows, straight) + exact_nt(im_rows, crossed)
        turned = jnp.concatenate([-im_rows, re_rows], axis=0)
        mirror = exact_nt(straight[0:8], rowed) + exact_nt(straight[8:16], turned)
        parts[taus[u], cores[u], 0:8, 0:16] = plain
        parts[taus[u], cores[u], 8:16, 0:16] = mirror

    for u in range(UNITS):
        trace(u)

    part_copies = []
    for step in range(1, 8):
        to = lax.rem(snk + step, 8)
        copy = pltpu.make_async_remote_copy(
            src_ref=parts.at[to], dst_ref=sums.at[step], send_sem=part_send.at[step],
            recv_sem=part_recv.at[step], device_id=(src, to), device_id_type=MESH,
        )
        copy.start()
        part_copies.append(copy)
    sums[0] = parts[snk]
    for copy in part_copies:
        copy.wait()
    sums[0] = jnp.sum(sums[...], axis=0)
    def swap_copy(c):
        return pltpu.make_async_remote_copy(
            src_ref=sums.at[0, c], dst_ref=swapped.at[core], send_sem=swap_send.at[c],
            recv_sem=swap_recv.at[core], device_id=(snk * 2 + c, tau), device_id_type=MESH,
        )

    @pl.when(outside)
    def _():
        for c in range(2):
            swap_copy(c).start()
        for c in range(2):
            swap_copy(c).wait_send()
            pltpu.make_async_remote_copy(
                src_ref=sums.at[0, c], dst_ref=swapped.at[c], send_sem=swap_send.at[c],
                recv_sem=swap_recv.at[c], device_id=(snk * 2 + c, tau), device_id_type=MESH,
            ).wait_recv()

    for c in range(2):
        value = sums[0, c, 0:8, :] + swapped[c, 8:16, :]
        out[0, 0, c] = value[:, 0:8]
        out[1, 0, c] = value[:, 8:16]
    for copy in sent:
        copy.wait_send()
    half_copy(mine).wait_send()


def on_device(perambulators, elements):
    ops, rows, width = elements.shape[1], elements.shape[3], elements.shape[4]
    bf16, f32 = jnp.bfloat16, jnp.float32
    copies = 20
    return pl.pallas_call(
        kernel,
        out_shape=jax.ShapeDtypeStruct((2, 1, 2, ops, ops), f32),
        in_specs=[pl.BlockSpec(memory_space=pl.ANY)] * 2,
        out_specs=pl.BlockSpec(memory_space=pltpu.VMEM),
        scratch_shapes=[
            pltpu.VMEM((ops, 2, width, width), bf16),
            pltpu.VMEM((9, ops, 2, rows, width), bf16),
            pltpu.VMEM((UNITS, 2, width, width), bf16),
            pltpu.VMEM((2, UNITS, 2, rows, width), bf16),
            pltpu.VMEM((UNITS, 2, ops, rows, width), bf16),
            pltpu.VMEM((UNITS, 2, ops, rows, width), bf16),
            pltpu.VMEM((8, 2, 16, 128), f32),
            pltpu.VMEM((8, 2, 16, 128), f32),
            pltpu.VMEM((2, 16, 128), f32),
            pltpu.SemaphoreType.DMA((UNITS + 1,)),
            pltpu.SemaphoreType.DMA((copies,)),
            pltpu.SemaphoreType.DMA((copies,)),
            pltpu.SemaphoreType.DMA((8,)),
            pltpu.SemaphoreType.DMA((8,)),
            pltpu.SemaphoreType.DMA((2,)),
            pltpu.SemaphoreType.DMA((2,)),
        ],
        compiler_params=pltpu.CompilerParams(
            collective_id=0, has_side_effects=True, vmem_limit_bytes=62 * 2**20
        ),
        cost_estimate=pl.CostEstimate(
            flops=20 * 10**9, bytes_accessed=12 * 2**20, transcendentals=0
        ),
        name="correlate",
    )(perambulators, elements)


def solution(mesh):
    placed = (P("src", None, None, None, None), P("src", None, None, "snk", None))
    return jax.shard_map(
        on_device,
        mesh=mesh,
        in_specs=placed,
        out_specs=P(None, "src", "snk", None, None),
        check_vma=False,
    )
```

profile of v0, /device:TPU:11, one launch (start us, length us, event | category | flops | bytes accessed | tf_op | source)
XLA Modules:
  0.0 122.6 jit_solution(9074642718037430583)
XLA Ops:
  0.0 121.3 %correlate.1 = f32[2,1,2,8,8]{4,3,2,1,0:T(8,128)} custom-call(bf16[1,16,2,512,512]{4,3,2,1,0:T(8,128)(2,1)} %peram.1, bf16[1,8,2,64,512]{4,3,2,1,0:T(8,128)(2,1)} %elem.1), custom_call_target="tpu_custom_call" | custom-call | flops 20000000000 | bytes 12582912 | tf_op jit(solution)/shard_map/correlate/pallas_call | solution.py:353
  121.3 1.3 %copy.4 = f32[2,1,2,8,8]{4,3,2,1,0:T(8,128)} copy(f32[2,1,2,8,8]{4,3,2,1,0:T(8,128)} %correlate.1) | data formatting | bytes 2048
where the time goes:
time: 125 us; the launch traced here: 123 us
  Pallas kernels  121 us (97%)
  local copies, waits for them, and re-layouts  1.32 us (1%)
    pallas_call x1, Pallas kernels, on_device(): pl.pallas_call(kernel, out_shape=jax.ShapeDtypeStruct((2, 1, 2, ops, ops)...  121 us

commit v1 on v0

--- a/solution.py
+++ b/solution.py
@@ -28,7 +28,7 @@
 
 
 def kernel(
-    peram, elem, out, full, other, mats, left, xs, ys, parts, sums, swapped,
+    peram, elem, out, full, other, mats, left, xs, ys, gram, rowed, parts, sums, swapped,
     load_sem, send_sem, recv_sem, part_send, part_recv, swap_send, swap_recv,
 ):
     src = lax.axis_index("src")
@@ -150,13 +150,57 @@
         start = pl.multiple_of((px * 2 + pyh) * rows, rows)
         return full.at[pl.ds(first, count), :, pl.ds(start, rows), :]
 
+    half = ops // 2
+    lower, upper = (0, half), (half, half)
+
+    def cut(ref, piece):
+        return ref.at[pl.ds(*piece)]
+
     mine = elem.at[0]
-    half = ops // 2
-    k_flip = remote(mine, other.at[FLIP], dev_flip)
-    k_xr = remote(mine, rows_of(x, yhi), dev_xr)
-    k_xl = remote(mine, rows_of(x, yhi), dev_xl)
-    k_yo = remote(mine, rows_of(x, yhi), dev_yo)
+    k_half = counter[0]
+    counter[0] += 1
+
+    def half_copy(source):
+        return pltpu.make_async_remote_copy(
+            src_ref=source, dst_ref=other.at[HALF], send_sem=send_sem.at[k_half],
+            recv_sem=recv_sem.at[k_half], device_id=dev_zo, device_id_type=MESH,
+        )
+
+    def to_both_sides(source, pyh):
+        sends = {}
+        for piece, device in (
+            (upper, dev_xr), (lower, dev_xl), (lower, dev_xr), (upper, dev_xl)
+        ):
+            sends[piece, device is dev_xr] = remote(
+                cut(source, piece), rows_of(x, pyh, *piece), device
+            )
+        return sends
+
+    def pass_on(sends, pyh):
+        arrived(sends[upper, True], rows_of(xl, pyh, *upper))
+        on_right = remote(rows_of(xl, pyh, *upper), rows_of(xl, pyh, *upper), dev_xr)
+        arrived(sends[lower, False], rows_of(xr, pyh, *lower))
+        on_left = remote(rows_of(xr, pyh, *lower), rows_of(xr, pyh, *lower), dev_xl)
+        return on_right, on_left
+
+    def rest_arrived(sends, pyh):
+        arrived(sends[lower, True], rows_of(xl, pyh, *lower))
+        arrived(sends[upper, False], rows_of(xr, pyh, *upper))
+
+    def passed_arrived(ks, pyh):
+        arrived(ks[0], rows_of(xo, pyh, *upper))
+        arrived(ks[1], rows_of(xo, pyh, *lower))
+
+    k_flip = [
+        remote(cut(mine, piece), cut(other.at[FLIP], piece), dev_flip) for piece in (lower, upper)
+    ]
+    own_sends = to_both_sides(mine, yhi)
     k_next = remote(mine, other.at[NEXT], dev_zp)
+
+    @pl.when(jnp.logical_not(low))
+    def _():
+        half_copy(mine).start()
+
     k_sib = remote(mine, other.at[SIB_OWN], dev_sib)
 
     col = lax.broadcasted_iota(jnp.int32, (rows, 512), 1)
@@ -173,8 +217,6 @@
         left[1, u, 1] = re.astype(jnp.bfloat16)
 
     def sink_product(u):
-        prepare(u)
-
         def tile(n, carry):
             cols = pl.ds(pl.multiple_of(n * 256, 256), 256)
             if u == 0:
@@ -196,89 +238,131 @@
 
         lax.fori_loop(0, 2, tile, 0)
 
-    def source_product(px):
+    lane = lax.broadcasted_iota(jnp.int32, (384, 128), 1)
+
+    def source_product(px, pyh, first):
         cols = pl.ds(pl.multiple_of(px * 128, 128), 128)
+        krows = pl.ds(pl.multiple_of((px * 2 + pyh) * rows, rows), rows)
+        here = (lane // 64) == pyh
 
         def tile(q, carry):
-            o = q * 2
-            wr = full[pl.ds(o, 2), 0, cols, :].reshape(256, 512)
-            wi = full[pl.ds(o, 2), 1, cols, :].reshape(256, 512)
+            wr = full[pl.ds(q * 4, 4), 0, krows, :].reshape(256, 512)
+            wi = full[pl.ds(q * 4, 4), 1, krows, :].reshape(256, 512)
             for m in range(3):
-                a = left[0, 3 * m : 3 * m + 3].reshape(384, 512)
-                b = left[1, 3 * m : 3 * m + 3].reshape(384, 512)
-                r = (dot_nt(a, wr) + dot_nt(b, wi)).astype(jnp.bfloat16)
-                ys[3 * m : 3 * m + 3, :, o, :, cols] = r[:, :128].reshape(3, 2, rows, 128)
-                ys[3 * m : 3 * m + 3, :, o + 1, :, cols] = r[:, 128:].reshape(3, 2, rows, 128)
+                units = slice(3 * m, 3 * m + 3)
+                a = left[0, units].reshape(384, 512)
+                b = left[1, units].reshape(384, 512)
+                r = dot_nt(a, wr) + dot_nt(b, wi)
+                for j in range(2):
+                    v = r[:, 128 * j : 128 * j + 128]
+                    w = pltpu.roll(v, 64, 1)
+                    for k, new in enumerate(
+                        (jnp.where(lane < 64, v, w), jnp.where(lane < 64, w, v))
+                    ):
+                        o = q * 4 + 2 * j + k
+                        if not first:
+                            old = ys[units, :, o, :, cols].reshape(384, 128)
+                            new = jnp.where(here, new, old.astype(jnp.float32))
+                        ys[units, :, o, :, cols] = new.astype(jnp.bfloat16).reshape(
+                            3, 2, rows, 128
+                        )
             return carry
 
-        lax.fori_loop(0, ops // 2, tile, 0)
+        lax.fori_loop(0, 2, tile, 0)
+
+    r_iota = lax.broadcasted_iota(jnp.int32, (256, 256), 0)
+    c_iota = lax.broadcasted_iota(jnp.int32, (256, 256), 1)
+    same = lax.rem(r_iota, 16) == lax.rem(c_iota, 16)
+
+    def trace(columns, last):
+        def unit(u, carry):
+            total = None
+            for s in range(rows // 16):
+                picked = []
+                for held in (xs, ys):
+                    picked.append(jnp.concatenate(
+                        [
+                            held[u, :, :, 16 * s : 16 * s + 16,
+                                 pl.ds(pl.multiple_of(px * 128, 128), 128)].reshape(256, 128)
+                            for px in columns
+                        ],
+                        axis=1,
+                    ))
+                product = dot_nt(*picked)
+                total = product if total is None else total + product
+            if last:
+                total = jnp.where(same, total + gram[u], 0.0)
+                rowed[u] = jnp.sum(total.reshape(2 * ops, 16, 256), axis=1)
+            else:
+                gram[u] = total
+            return carry
+
+        lax.fori_loop(0, UNITS, unit, 0)
 
     own_load.wait()
+    for u in range(UNITS):
+        prepare(u)
     sink_product(0)
-    arrived(k_flip, other.at[FLIP])
-    k_prev = remote(other.at[FLIP], other.at[FLIP_PREV], dev_zn)
-    k_half = counter[0]
-    counter[0] += 1
-
-    def half_copy(source):
-        return pltpu.make_async_remote_copy(
-            src_ref=source, dst_ref=other.at[HALF], send_sem=send_sem.at[k_half],
-            recv_sem=recv_sem.at[k_half], device_id=dev_zo, device_id_type=MESH,
-        )
+    k_yo, k_prev = [], []
+
+    def relay(i, piece):
+        arrived(k_flip[i], cut(other.at[FLIP], piece))
+        k_yo.append(
+            remote(cut(other.at[FLIP], piece), rows_of(x, y_from // 2, *piece), dev_flip)
+        )
+        k_prev.append(
+            remote(cut(other.at[FLIP], piece), cut(other.at[FLIP_PREV], piece), dev_zn)
+        )
+
+    relay(0, lower)
+    source_product(x, yhi, True)
+    relay(1, upper)
 
     @pl.when(low)
     def _():
         half_copy(other.at[FLIP]).start()
 
-    @pl.when(jnp.logical_not(low))
-    def _():
-        half_copy(mine).start()
-
     k_sib_flip = remote(other.at[FLIP], other.at[SIB_FLIP], dev_sib)
     arrived(k_sib, other.at[SIB_OWN])
     sink_product(1)
+    own_passed = pass_on(own_sends, yhi)
     arrived(k_sib_flip, other.at[SIB_FLIP])
     sink_product(2)
-
-    def forward(k_from_left, k_from_right, pyh):
-        arrived(k_from_left, rows_of(xl, pyh))
-        on_right = remote(rows_of(xl, pyh, half, half), rows_of(xl, pyh, half, half), dev_xr)
-        arrived(k_from_right, rows_of(xr, pyh))
-        on_left = remote(rows_of(xr, pyh, 0, half), rows_of(xr, pyh, 0, half), dev_xl)
-        return on_right, on_left
-
-    own_right, own_left = forward(k_xr, k_xl, yhi)
-    arrived(k_yo, rows_of(x, yoh))
-    k_oxr = remote(rows_of(x, yoh), rows_of(x, yoh), dev_xr)
-    k_oxl = remote(rows_of(x, yoh), rows_of(x, yoh), dev_xl)
+    arrived(k_yo[0], rows_of(x, yoh, *lower))
+    arrived(k_yo[1], rows_of(x, yoh, *upper))
+    other_sends = to_both_sides(rows_of(x, yoh), yoh)
+    source_product(x, yoh, False)
+    rest_arrived(own_sends, yhi)
+    source_product(xl, yhi, True)
+    source_product(xr, yhi, True)
     arrived(k_next, other.at[NEXT])
     k_sib_next = remote(other.at[NEXT], other.at[SIB_NEXT], dev_sib)
     sink_product(3)
     arrived(k_sib_next, other.at[SIB_NEXT])
     sink_product(4)
-    arrived(k_prev, other.at[FLIP_PREV])
+    passed_arrived(own_passed, yhi)
+    source_product(xo, yhi, True)
+    arrived(k_prev[0], cut(other.at[FLIP_PREV], lower))
+    arrived(k_prev[1], cut(other.at[FLIP_PREV], upper))
     k_sib_prev = remote(other.at[FLIP_PREV], other.at[SIB_FLIP_PREV], dev_sib)
     sink_product(5)
     arrived(k_sib_prev, other.at[SIB_FLIP_PREV])
     sink_product(6)
+    other_passed = pass_on(other_sends, yoh)
     arrived(k_half, other.at[HALF])
     k_sib_half = remote(other.at[HALF], other.at[SIB_HALF], dev_sib)
     sink_product(7)
     arrived(k_sib_half, other.at[SIB_HALF])
     sink_product(8)
-    source_product(x)
-    other_right, other_left = forward(k_oxr, k_oxl, yoh)
-    source_product(xl)
-    source_product(xr)
-    for k_right, k_left, pyh in ((own_right, own_left, yhi), (other_right, other_left, yoh)):
-        arrived(k_right, rows_of(xo, pyh, half, half))
-        arrived(k_left, rows_of(xo, pyh, 0, half))
-    source_product(xo)
+    rest_arrived(other_sends, yoh)
+    source_product(xl, yoh, False)
+    source_product(xr, yoh, False)
+    trace((x, xl, xr), False)
+    passed_arrived(other_passed, yoh)
+    source_product(xo, yoh, False)
+    trace((xo,), True)
 
     parts[...] = jnp.zeros_like(parts)
-    r_iota = lax.broadcasted_iota(jnp.int32, (256, 256), 0)
-    c_iota = lax.broadcasted_iota(jnp.int32, (256, 256), 1)
-    same = lax.rem(r_iota, 16) == lax.rem(c_iota, 16)
     pick_row = lax.broadcasted_iota(jnp.int32, (16, 256), 0)
     pick_group = lax.broadcasted_iota(jnp.int32, (16, 256), 1) // 16
     straight = jnp.where(pick_row == pick_group, 1.0, 0.0)
@@ -287,25 +371,11 @@
         jnp.where(pick_group == pick_row + 8, -1.0, 0.0),
         jnp.where(pick_group == pick_row - 8, 1.0, 0.0),
     )
-
-    def trace(u):
-        total = jnp.zeros((256, 256), jnp.float32)
-        for s in range(rows // 16):
-            a = xs[u, :, :, 16 * s : 16 * s + 16, :].reshape(256, 512)
-            b = ys[u, :, :, 16 * s : 16 * s + 16, :].reshape(256, 512)
-            total += dot_nt(a, b)
-        total = jnp.where(same, total, 0.0)
-        rowed = jnp.sum(total.reshape(16, 16, 256), axis=1)
-        re_rows = rowed[0:8]
-        im_rows = rowed[8:16]
-        plain = exact_nt(re_rows, straight) + exact_nt(im_rows, crossed)
-        turned = jnp.concatenate([-im_rows, re_rows], axis=0)
-        mirror = exact_nt(straight[0:8], rowed) + exact_nt(straight[8:16], turned)
-        parts[taus[u], cores[u], 0:8, 0:16] = plain
-        parts[taus[u], cores[u], 8:16, 0:16] = mirror
-
+    traces = exact_nt(rowed[:, 0:8].reshape(UNITS * 8, 256), straight) + exact_nt(
+        rowed[:, 8:16].reshape(UNITS * 8, 256), crossed
+    )
     for u in range(UNITS):
-        trace(u)
+        parts[taus[u], cores[u], :, 0:16] = traces[8 * u : 8 * u + 8]
 
     part_copies = []
     for step in range(1, 8):
@@ -337,10 +407,12 @@
                 recv_sem=swap_recv.at[c], device_id=(snk * 2 + c, tau), device_id_type=MESH,
             ).wait_recv()
 
+    turn_row = lax.broadcasted_iota(jnp.int32, (8, 128), 0)
+    turn_lane = lax.broadcasted_iota(jnp.int32, (8, 128), 1)
     for c in range(2):
-        value = sums[0, c, 0:8, :] + swapped[c, 8:16, :]
-        out[0, 0, c] = value[:, 0:8]
-        out[1, 0, c] = value[:, 8:16]
+        for part in range(2):
+            turn = jnp.where(turn_lane == turn_row + 8 * part, 1.0, 0.0)
+            out[part, 0, c] = sums[0, c, :, 8 * part : 8 * part + 8] + exact_nt(turn, swapped[c])
     for copy in sent:
         copy.wait_send()
     half_copy(mine).wait_send()
@@ -349,7 +421,7 @@
 def on_device(perambulators, elements):
     ops, rows, width = elements.shape[1], elements.shape[3], elements.shape[4]
     bf16, f32 = jnp.bfloat16, jnp.float32
-    copies = 20
+    copies = 32
     return pl.pallas_call(
         kernel,
         out_shape=jax.ShapeDtypeStruct((2, 1, 2, ops, ops), f32),
@@ -362,9 +434,11 @@
             pltpu.VMEM((2, UNITS, 2, rows, width), bf16),
             pltpu.VMEM((UNITS, 2, ops, rows, width), bf16),
             pltpu.VMEM((UNITS, 2, ops, rows, width), bf16),
-            pltpu.VMEM((8, 2, 16, 128), f32),
-            pltpu.VMEM((8, 2, 16, 128), f32),
-            pltpu.VMEM((2, 16, 128), f32),
+            pltpu.VMEM((UNITS, 256, 256), f32),
+            pltpu.VMEM((UNITS, 16, 256), f32),
+            pltpu.VMEM((8, 2, 8, 128), f32),
+            pltpu.VMEM((8, 2, 8, 128), f32),
+            pltpu.VMEM((2, 8, 128), f32),
             pltpu.SemaphoreType.DMA((UNITS + 1,)),
             pltpu.SemaphoreType.DMA((copies,)),
             pltpu.SemaphoreType.DMA((copies,)),

time: 125 us -> 95.4 us (0.76); the launches traced: 123 us -> 95.1 us
  Pallas kernels: 121 us -> 93.8 us
    pallas_call x1, Pallas kernels: 121 us -> 93.8 us  [on_device(): pl.pallas_call(kernel, out_shape=jax.ShapeDtypeStruct((2, 1, 2, ops, ops)...]
where the time goes in v1:
time: 95.4 us; the launch traced here: 95.1 us
  Pallas kernels  93.8 us (98%)
  local copies, waits for them, and re-layouts  1.32 us (1%)
    pallas_call x1, Pallas kernels, on_device(): pl.pallas_call(kernel, out_shape=jax.ShapeDtypeStruct((2, 1, 2, ops, ops)...  93.8 us

profile of v1, /device:TPU:11, one launch (start us, length us, event | category | flops | bytes accessed | tf_op | source)
XLA Modules:
  0.0 95.1 jit_solution(17192171870007252163)
XLA Ops:
  0.0 93.8 %correlate.1 = f32[2,1,2,8,8]{4,3,2,1,0:T(8,128)} custom-call(bf16[1,16,2,512,512]{4,3,2,1,0:T(8,128)(2,1)} %peram.1, bf16[1,8,2,64,512]{4,3,2,1,0:T(8,128)(2,1)} %elem.1), custom_call_target="tpu_custom_call" | custom-call | flops 20000000000 | bytes 12582912 | tf_op jit(solution)/shard_map/correlate/pallas_call | solution.py:425
  93.8 1.3 %copy.4 = f32[2,1,2,8,8]{4,3,2,1,0:T(8,128)} copy(f32[2,1,2,8,8]{4,3,2,1,0:T(8,128)} %correlate.1) | data formatting | bytes 2048

commit v2 on v1

--- a/solution.py
+++ b/solution.py
@@ -46,8 +46,8 @@
     def place(px, py, pz, pc):
         return ((lax.rem(py, 2) * 4 + pz) * 2 + pc, px * 2 + py // 2)
 
-    xr = lax.rem(x + 1, 4)
-    xl = lax.rem(x + 3, 4)
+    xf = lax.rem(x + 1 + 2 * core, 4)
+    xb = lax.rem(x + 3 + 2 * core, 4)
     xo = lax.rem(x + 2, 4)
     yn = lax.rem(y + 1, 4)
     yp = lax.rem(y + 3, 4)
@@ -56,8 +56,8 @@
     zp = lax.rem(z + 3, 4)
     zo = lax.rem(z + 2, 4)
     yoh = yo // 2
-    dev_xr = place(xr, y, z, core)
-    dev_xl = place(xl, y, z, core)
+    dev_fore = place(xf, y, z, core)
+    dev_back = place(xb, y, z, core)
     dev_yo = place(x, yo, z, core)
     y_to = lax.rem(y + 3 + 2 * core, 4)
     y_from = lax.rem(y + 1 + 2 * core, 4)
@@ -150,8 +150,9 @@
         start = pl.multiple_of((px * 2 + pyh) * rows, rows)
         return full.at[pl.ds(first, count), :, pl.ds(start, rows), :]
 
-    half = ops // 2
-    lower, upper = (0, half), (half, half)
+    quarters = ((0, 2), (2, 2), (4, 2), (6, 2))
+    tail, fifth, head = (5, 3), (4, 1), (0, 4)
+    pair, triple = (0, 2), (2, 3)
 
     def cut(ref, piece):
         return ref.at[pl.ds(*piece)]
@@ -166,35 +167,14 @@
             recv_sem=recv_sem.at[k_half], device_id=dev_zo, device_id_type=MESH,
         )
 
-    def to_both_sides(source, pyh):
-        sends = {}
-        for piece, device in (
-            (upper, dev_xr), (lower, dev_xl), (lower, dev_xr), (upper, dev_xl)
-        ):
-            sends[piece, device is dev_xr] = remote(
-                cut(source, piece), rows_of(x, pyh, *piece), device
-            )
-        return sends
-
-    def pass_on(sends, pyh):
-        arrived(sends[upper, True], rows_of(xl, pyh, *upper))
-        on_right = remote(rows_of(xl, pyh, *upper), rows_of(xl, pyh, *upper), dev_xr)
-        arrived(sends[lower, False], rows_of(xr, pyh, *lower))
-        on_left = remote(rows_of(xr, pyh, *lower), rows_of(xr, pyh, *lower), dev_xl)
-        return on_right, on_left
-
-    def rest_arrived(sends, pyh):
-        arrived(sends[lower, True], rows_of(xl, pyh, *lower))
-        arrived(sends[upper, False], rows_of(xr, pyh, *upper))
-
-    def passed_arrived(ks, pyh):
-        arrived(ks[0], rows_of(xo, pyh, *upper))
-        arrived(ks[1], rows_of(xo, pyh, *lower))
-
-    k_flip = [
-        remote(cut(mine, piece), cut(other.at[FLIP], piece), dev_flip) for piece in (lower, upper)
-    ]
-    own_sends = to_both_sides(mine, yhi)
+    def block(px, pyh, piece):
+        return rows_of(px, pyh, *piece)
+
+    k_flip = [remote(cut(mine, q), cut(other.at[FLIP], q), dev_flip) for q in quarters]
+    k_own_fore, k_own_back = {}, {}
+    for piece in (tail, fifth, head):
+        k_own_fore[piece] = remote(cut(mine, piece), block(x, yhi, piece), dev_fore)
+        k_own_back[piece] = remote(cut(mine, piece), block(x, yhi, piece), dev_back)
     k_next = remote(mine, other.at[NEXT], dev_zp)
 
     @pl.when(jnp.logical_not(low))
@@ -305,60 +285,95 @@
     sink_product(0)
     k_yo, k_prev = [], []
 
-    def relay(i, piece):
-        arrived(k_flip[i], cut(other.at[FLIP], piece))
-        k_yo.append(
-            remote(cut(other.at[FLIP], piece), rows_of(x, y_from // 2, *piece), dev_flip)
-        )
-        k_prev.append(
-            remote(cut(other.at[FLIP], piece), cut(other.at[FLIP_PREV], piece), dev_zn)
-        )
-
-    relay(0, lower)
+    def relay(i):
+        q = quarters[i]
+        arrived(k_flip[i], cut(other.at[FLIP], q))
+        k_yo.append(remote(cut(other.at[FLIP], q), block(x, y_from // 2, q), dev_flip))
+        k_prev.append(remote(cut(other.at[FLIP], q), cut(other.at[FLIP_PREV], q), dev_zn))
+
+    def partner(i):
+        arrived(k_yo[i], block(x, yoh, quarters[i]))
+
+    def partner_send(piece):
+        mine_too = block(x, yoh, piece)
+        if piece is pair:
+            k_part_fore[piece] = remote(mine_too, mine_too, dev_fore)
+            k_part_back[piece] = remote(mine_too, mine_too, dev_back)
+        else:
+            k_part_back[piece] = remote(mine_too, mine_too, dev_back)
+            k_part_fore[piece] = remote(mine_too, mine_too, dev_fore)
+
+    relay(0)
+    relay(1)
     source_product(x, yhi, True)
-    relay(1, upper)
+    relay(2)
+    relay(3)
 
     @pl.when(low)
     def _():
         half_copy(other.at[FLIP]).start()
 
     k_sib_flip = remote(other.at[FLIP], other.at[SIB_FLIP], dev_sib)
+    arrived(k_own_fore[tail], block(xb, yhi, tail))
+    k_pass_tail = remote(block(xb, yhi, tail), block(xb, yhi, tail), dev_fore)
+    k_cross_b = remote(block(xb, yhi, tail), block(xb, yhi, tail), dev_yo)
+    arrived(k_own_back[tail], block(xf, yhi, tail))
+    k_cross_f = remote(block(xf, yhi, tail), block(xf, yhi, tail), dev_yo)
     arrived(k_sib, other.at[SIB_OWN])
     sink_product(1)
-    own_passed = pass_on(own_sends, yhi)
     arrived(k_sib_flip, other.at[SIB_FLIP])
     sink_product(2)
-    arrived(k_yo[0], rows_of(x, yoh, *lower))
-    arrived(k_yo[1], rows_of(x, yoh, *upper))
-    other_sends = to_both_sides(rows_of(x, yoh), yoh)
+    k_part_fore, k_part_back = {}, {}
+    partner(0)
+    partner_send(pair)
+    partner(1)
+    partner(2)
+    partner_send(triple)
+    arrived(k_own_fore[fifth], block(xb, yhi, fifth))
+    k_pass_fifth = remote(block(xb, yhi, fifth), block(xb, yhi, fifth), dev_fore)
+    arrived(k_own_back[head], block(xf, yhi, head))
+    k_pass_head = remote(block(xf, yhi, head), block(xf, yhi, head), dev_back)
+    partner(3)
     source_product(x, yoh, False)
-    rest_arrived(own_sends, yhi)
-    source_product(xl, yhi, True)
-    source_product(xr, yhi, True)
+    arrived(k_own_fore[head], block(xb, yhi, head))
+    source_product(xb, yhi, True)
+    arrived(k_pass_tail, block(xo, yhi, tail))
+    k_cross_o = remote(block(xo, yhi, tail), block(xo, yhi, tail), dev_yo)
+    arrived(k_own_back[fifth], block(xf, yhi, fifth))
+    source_product(xf, yhi, True)
     arrived(k_next, other.at[NEXT])
     k_sib_next = remote(other.at[NEXT], other.at[SIB_NEXT], dev_sib)
     sink_product(3)
     arrived(k_sib_next, other.at[SIB_NEXT])
     sink_product(4)
-    passed_arrived(own_passed, yhi)
-    source_product(xo, yhi, True)
-    arrived(k_prev[0], cut(other.at[FLIP_PREV], lower))
-    arrived(k_prev[1], cut(other.at[FLIP_PREV], upper))
+    for i, q in enumerate(quarters):
+        arrived(k_prev[i], cut(other.at[FLIP_PREV], q))
     k_sib_prev = remote(other.at[FLIP_PREV], other.at[SIB_FLIP_PREV], dev_sib)
     sink_product(5)
+    arrived(k_part_fore[pair], block(xb, yoh, pair))
+    k_pass_pair = remote(block(xb, yoh, pair), block(xb, yoh, pair), dev_fore)
     arrived(k_sib_prev, other.at[SIB_FLIP_PREV])
     sink_product(6)
-    other_passed = pass_on(other_sends, yoh)
+    arrived(k_part_back[triple], block(xf, yoh, triple))
+    k_pass_triple = remote(block(xf, yoh, triple), block(xf, yoh, triple), dev_back)
+    arrived(k_pass_fifth, block(xo, yhi, fifth))
+    arrived(k_pass_head, block(xo, yhi, head))
+    source_product(xo, yhi, True)
     arrived(k_half, other.at[HALF])
     k_sib_half = remote(other.at[HALF], other.at[SIB_HALF], dev_sib)
     sink_product(7)
     arrived(k_sib_half, other.at[SIB_HALF])
     sink_product(8)
-    rest_arrived(other_sends, yoh)
-    source_product(xl, yoh, False)
-    source_product(xr, yoh, False)
-    trace((x, xl, xr), False)
-    passed_arrived(other_passed, yoh)
+    arrived(k_part_fore[triple], block(xb, yoh, triple))
+    arrived(k_cross_b, block(xb, yoh, tail))
+    source_product(xb, yoh, False)
+    arrived(k_part_back[pair], block(xf, yoh, pair))
+    arrived(k_cross_f, block(xf, yoh, tail))
+    source_product(xf, yoh, False)
+    trace((x, xf, xb), False)
+    arrived(k_cross_o, block(xo, yoh, tail))
+    arrived(k_pass_pair, block(xo, yoh, pair))
+    arrived(k_pass_triple, block(xo, yoh, triple))
     source_product(xo, yoh, False)
     trace((xo,), True)
 
@@ -421,7 +436,7 @@
 def on_device(perambulators, elements):
     ops, rows, width = elements.shape[1], elements.shape[3], elements.shape[4]
     bf16, f32 = jnp.bfloat16, jnp.float32
-    copies = 32
+    copies = 48
     return pl.pallas_call(
         kernel,
         out_shape=jax.ShapeDtypeStruct((2, 1, 2, ops, ops), f32),

time: 95.4 us -> 102 us (1.069); the launches traced: 95.1 us -> 99.9 us
  Pallas kernels: 93.8 us -> 98.6 us
    pallas_call x1, Pallas kernels: 93.8 us -> 98.6 us  [on_device(): pl.pallas_call(kernel, out_shape=jax.ShapeDtypeStruct((2, 1, 2, ops, ops)...]
where the time goes in v2:
time: 102 us; the launch traced here: 99.9 us
  Pallas kernels  98.6 us (97%)
  local copies, waits for them, and re-layouts  1.32 us (1%)
    pallas_call x1, Pallas kernels, on_device(): pl.pallas_call(kernel, out_shape=jax.ShapeDtypeStruct((2, 1, 2, ops, ops)...  98.6 us

profile of v2, /device:TPU:11, one launch (start us, length us, event | category | flops | bytes accessed | tf_op | source)
XLA Modules:
  0.0 99.9 jit_solution(15530051802265272031)
XLA Ops:
  0.0 98.6 %correlate.1 = f32[2,1,2,8,8]{4,3,2,1,0:T(8,128)} custom-call(bf16[1,16,2,512,512]{4,3,2,1,0:T(8,128)(2,1)} %peram.1, bf16[1,8,2,64,512]{4,3,2,1,0:T(8,128)(2,1)} %elem.1), custom_call_target="tpu_custom_call" | custom-call | flops 20000000000 | bytes 12582912 | tf_op jit(solution)/shard_map/correlate/pallas_call | solution.py:440
  98.6 1.3 %copy.4 = f32[2,1,2,8,8]{4,3,2,1,0:T(8,128)} copy(f32[2,1,2,8,8]{4,3,2,1,0:T(8,128)} %correlate.1) | data formatting | bytes 2048

commit v3 on v2

v3 whole, which is shorter than its diff:
```python
import jax
import jax.numpy as jnp
from jax import lax
from jax.experimental import pallas as pl
from jax.experimental.pallas import tpu as pltpu
from jax.sharding import PartitionSpec as P

MESH = pl.DeviceIdType.MESH
UNITS = 9
NT_DIMS = (((1,), (1,)), ((), ()))

FLIP, NEXT, FLIP_PREV, HALF = 0, 1, 2, 3
SIB_OWN, SIB_FLIP, SIB_NEXT, SIB_FLIP_PREV, SIB_HALF = 4, 5, 6, 7, 8


ORDER = (
    "flip0", "flip1", "flip2", "flip3", "fore_tail", "back_tail", "fore_fifth", "back_fifth",
    "fore_head", "back_head", "next", "half_own", "sib", "S0", "Yx1", "S1", "pass_fifth",
    "yo0", "prev0", "yo1", "prev1", "yo2", "prev2", "yo3", "prev3", "half_flip", "sib_flip",
    "S2", "cross_b", "pass_tail", "cross_f", "fore_pair", "back_pair", "Yb1", "pass_head",
    "back_triple", "fore_triple", "Yx2", "Yf1", "sib_next", "S3", "sib_prev", "S5", "S4",
    "pass_pair", "S6", "cross_o", "sib_half", "S7", "pass_triple", "Yb2", "S8", "Yo1",
    "Yf2", "T1", "Yo2", "T2",
)


def dot(a, b):
    return jnp.dot(a, b, preferred_element_type=jnp.float32)


def dot_nt(a, b):
    return lax.dot_general(a, b, NT_DIMS, preferred_element_type=jnp.float32)


def exact_nt(a, b):
    return lax.dot_general(
        a, b, NT_DIMS, preferred_element_type=jnp.float32, precision=lax.Precision.HIGHEST
    )


def kernel(
    peram, elem, out, full, other, mats, left, xs, ys, gram, rowed, parts, sums, swapped,
    load_sem, send_sem, recv_sem, part_send, part_recv, swap_send, swap_recv,
):
    src = lax.axis_index("src")
    snk = lax.axis_index("snk")
    core = lax.rem(src, 2)
    z = lax.rem(src // 2, 4)
    ylo = src // 8
    x = snk // 2
    yhi = lax.rem(snk, 2)
    y = yhi * 2 + ylo
    tau = src // 2
    ops = elem.shape[1]
    rows = elem.shape[3]

    def place(px, py, pz, pc):
        return ((lax.rem(py, 2) * 4 + pz) * 2 + pc, px * 2 + py // 2)

    xf = lax.rem(x + 1 + 2 * core, 4)
    xb = lax.rem(x + 3 + 2 * core, 4)
    xo = lax.rem(x + 2, 4)
    yn = lax.rem(y + 1, 4)
    yp = lax.rem(y + 3, 4)
    yo = lax.rem(y + 2, 4)
    zn = lax.rem(z + 1, 4)
    zp = lax.rem(z + 3, 4)
    zo = lax.rem(z + 2, 4)
    yoh = yo // 2
    dev_fore = place(xf, y, z, core)
    dev_back = place(xb, y, z, core)
    dev_yo = place(x, yo, z, core)
    y_to = lax.rem(y + 3 + 2 * core, 4)
    y_from = lax.rem(y + 1 + 2 * core, 4)
    y_from_sib = lax.rem(y + 3 + 2 * core, 4)
    dev_flip = place(x, y_to, z, core)
    dev_flip_back = place(x, y_from, z, core)
    dev_zn = place(x, y, zn, core)
    dev_zp = place(x, y, zp, core)
    dev_zo = place(x, y, zo, core)
    dev_sib = (src + 1 - 2 * core, snk)

    own_rows = snk
    flip_rows = x * 2 + y_from // 2
    flip_rows_sib = x * 2 + y_from_sib // 2
    low = z < 2
    flip_tau = (1 - ylo) * 4 + z
    next_tau = ylo * 4 + zn
    prev_tau = (1 - ylo) * 4 + zp
    half_tau = jnp.where(low, ylo, 1 - ylo) * 4 + zo
    sib = 1 - core
    flip_core = lax.rem(core + ylo, 2)
    taus = [tau, tau, flip_tau, next_tau, next_tau, prev_tau, prev_tau, half_tau, half_tau]
    cores = [core, sib, flip_core, core, sib, core, sib, core, sib]
    blocks = [
        own_rows,
        own_rows,
        jnp.where(ylo == 0, flip_rows, flip_rows_sib),
        own_rows,
        own_rows,
        flip_rows,
        flip_rows_sib,
        jnp.where(low, own_rows, flip_rows),
        jnp.where(low, own_rows, flip_rows_sib),
    ]
    slots = [
        None, SIB_OWN, jnp.where(ylo == 0, FLIP, SIB_FLIP), NEXT, SIB_NEXT,
        FLIP_PREV, SIB_FLIP_PREV, HALF, SIB_HALF,
    ]

    own_slice = full.at[:, :, pl.ds(pl.multiple_of(snk * rows, rows), rows), :]
    own_load = pltpu.make_async_copy(elem.at[0], own_slice, load_sem.at[UNITS])
    own_load.start()
    loads = []
    for u in range(UNITS):
        load = pltpu.make_async_copy(
            peram.at[0, taus[u] * 2 + cores[u]], mats.at[u], load_sem.at[u]
        )
        load.start()
        loads.append(load)

    swapped[...] = jnp.zeros_like(swapped)

    barrier = pltpu.get_barrier_semaphore()
    for step in range(1, 8):
        pl.semaphore_signal(
            barrier, inc=1, device_id=(src, lax.rem(snk + step, 8)), device_id_type=MESH
        )
    for target in (dev_flip, dev_flip_back, dev_zn, dev_zp, dev_zo, dev_sib):
        pl.semaphore_signal(barrier, inc=1, device_id=target, device_id_type=MESH)
    outside = snk != tau

    @pl.when(outside)
    def _():
        for c in range(2):
            pl.semaphore_signal(barrier, inc=1, device_id=(snk * 2 + c, tau), device_id_type=MESH)

    pl.semaphore_wait(barrier, jnp.where(outside, 15, 13))

    quarters = ((0, 2), (2, 2), (4, 2), (6, 2))
    tail, fifth, head = (5, 3), (4, 1), (0, 4)
    pair, triple = (0, 2), (2, 3)

    def block(px, pyh, piece):
        start = pl.multiple_of((px * 2 + pyh) * rows, rows)
        return full.at[pl.ds(*piece), :, pl.ds(start, rows), :]

    def slot(index, piece=(0, ops)):
        return other.at[index, pl.ds(*piece)]

    def mine(piece=(0, ops)):
        return elem.at[0, pl.ds(*piece)]

    sends = {}
    flips = tuple("flip%d" % i for i in range(4))
    prevs = tuple("prev%d" % i for i in range(4))
    partners = tuple("yo%d" % i for i in range(4))
    for i, q in enumerate(quarters):
        sends[flips[i]] = ((), mine(q), slot(FLIP, q), dev_flip, slot(FLIP, q))
        sends[partners[i]] = (
            flips[i : i + 1], slot(FLIP, q), block(x, y_from // 2, q), dev_flip,
            block(x, yoh, q),
        )
        sends[prevs[i]] = (
            flips[i : i + 1], slot(FLIP, q), slot(FLIP_PREV, q), dev_zn, slot(FLIP_PREV, q)
        )
    for name, piece in (("tail", tail), ("fifth", fifth), ("head", head)):
        sends["fore_" + name] = (
            (), mine(piece), block(x, yhi, piece), dev_fore, block(xb, yhi, piece)
        )
        sends["back_" + name] = (
            (), mine(piece), block(x, yhi, piece), dev_back, block(xf, yhi, piece)
        )
    for name, piece, needs in (
        ("pair", pair, partners[0:1]), ("triple", triple, partners[1:3])
    ):
        here = block(x, yoh, piece)
        sends["fore_" + name] = (needs, here, here, dev_fore, block(xb, yoh, piece))
        sends["back_" + name] = (needs, here, here, dev_back, block(xf, yoh, piece))
    for name, side, px, pyh, piece, device in (
        ("tail", "fore_", xb, yhi, tail, dev_fore),
        ("fifth", "fore_", xb, yhi, fifth, dev_fore),
        ("head", "back_", xf, yhi, head, dev_back),
        ("pair", "fore_", xb, yoh, pair, dev_fore),
        ("triple", "back_", xf, yoh, triple, dev_back),
    ):
        here = block(px, pyh, piece)
        sends["pass_" + name] = ((side + name,), here, here, device, block(xo, pyh, piece))
    for name, needs, px in (
        ("cross_b", "fore_tail", xb), ("cross_f", "back_tail", xf), ("cross_o", "pass_tail", xo)
    ):
        here = block(px, yhi, tail)
        sends[name] = ((needs,), here, here, dev_yo, block(px, yoh, tail))
    sends["next"] = ((), mine(), slot(NEXT), dev_zp, slot(NEXT))
    sends["half"] = ((), mine(), slot(HALF), dev_zo, slot(HALF))
    for name, needs, source, target in (
        ("sib", (), mine(), SIB_OWN),
        ("sib_flip", flips, slot(FLIP), SIB_FLIP),
        ("sib_next", ("next",), slot(NEXT), SIB_NEXT),
        ("sib_prev", prevs, slot(FLIP_PREV), SIB_FLIP_PREV),
        ("sib_half", ("half",), slot(HALF), SIB_HALF),
    ):
        sends[name] = (needs, source, slot(target), dev_sib, slot(target))
    numbers = {name: i for i, name in enumerate(sends)}
    seen = set()

    def descriptor(name, source, target, device):
        i = numbers[name]
        return pltpu.make_async_remote_copy(
            src_ref=source, dst_ref=target, send_sem=send_sem.at[i], recv_sem=recv_sem.at[i],
            device_id=device, device_id_type=MESH,
        )

    def arrive(names):
        for name in names:
            if name not in seen:
                seen.add(name)
                landed = sends[name][4]
                descriptor(name, landed, landed, dev_sib).wait_recv()

    def send(name):
        needs, source, target, device, _ = sends[name]
        arrive(needs)
        descriptor(name, source, target, device).start()

    def send_half(when, source):
        @pl.when(when)
        def _():
            descriptor("half", source, slot(HALF), dev_zo).start()

    col = lax.broadcasted_iota(jnp.int32, (rows, 512), 1)
    lane_sign = jnp.where(col < 256, 1.0, -1.0) * jnp.where(x < 2, 1.0, -1.0)

    def prepare(u):
        loads[u].wait()
        start = pl.multiple_of(blocks[u] * rows, rows)
        re = mats[u, 0, pl.ds(start, rows), :].astype(jnp.float32) * lane_sign
        im = mats[u, 1, pl.ds(start, rows), :].astype(jnp.float32) * lane_sign
        left[0, u, 0] = re.astype(jnp.bfloat16)
        left[0, u, 1] = (-im).astype(jnp.bfloat16)
        left[1, u, 0] = im.astype(jnp.bfloat16)
        left[1, u, 1] = re.astype(jnp.bfloat16)

    def sink_product(u):
        if u == 0:
            start = pl.multiple_of(snk * rows, rows)
            er = full[:, 0, pl.ds(start, rows), :]
            ei = full[:, 1, pl.ds(start, rows), :]
        else:
            er = other[slots[u], :, 0]
            ei = other[slots[u], :, 1]
        e = jnp.concatenate(
            [er.reshape(ops * rows, 512), ei.reshape(ops * rows, 512)], axis=1
        )
        pr = mats[u, 0]
        pi = mats[u, 1]
        re = dot(e, jnp.concatenate([pr, -pi], axis=0))
        xs[u, 0] = re.astype(jnp.bfloat16).reshape(ops, rows, 512)
        im = dot(e, jnp.concatenate([pi, pr], axis=0))
        xs[u, 1] = im.astype(jnp.bfloat16).reshape(ops, rows, 512)

    lane = lax.broadcasted_iota(jnp.int32, (384, 128), 1)

    def source_product(px, pyh, first):
        cols = pl.ds(pl.multiple_of(px * 128, 128), 128)
        krows = pl.ds(pl.multiple_of((px * 2 + pyh) * rows, rows), rows)
        here = (lane // 64) == pyh
        for m in range(3):
            units = slice(3 * m, 3 * m + 3)
            a = jnp.concatenate(
                [left[0, units].reshape(384, 512), left[1, units].reshape(384, 512)], axis=1
            )
            for q in range(ops // 4):
                w = jnp.concatenate(
                    [full[4 * q : 4 * q + 4, c, krows, :].reshape(256, 512) for c in range(2)],
                    axis=1,
                )
                r = dot_nt(a, w)
                for j in range(2):
                    v = r[:, 128 * j : 128 * j + 128]
                    t = pltpu.roll(v, 64, 1)
                    for k, new in enumerate(
                        (jnp.where(lane < 64, v, t), jnp.where(lane < 64, t, v))
                    ):
                        o = q * 4 + 2 * j + k
                        new = new.astype(jnp.bfloat16)
                        if not first:
                            new = jnp.where(here, new, ys[units, :, o, :, cols].reshape(384, 128))
                        ys[units, :, o, :, cols] = new.reshape(3, 2, rows, 128)

    r_iota = lax.broadcasted_iota(jnp.int32, (256, 256), 0)
    c_iota = lax.broadcasted_iota(jnp.int32, (256, 256), 1)
    same = lax.rem(r_iota, 16) == lax.rem(c_iota, 16)

    def trace(columns, last):
        for u in range(UNITS):
            total = dot_nt(*(
                jnp.concatenate(
                    [
                        held[u, :, :, 16 * i : 16 * i + 16,
                             pl.ds(pl.multiple_of(px * 128, 128), 128)].reshape(256, 128)
                        for i in range(rows // 16)
                        for px in columns
                    ],
                    axis=1,
                )
                for held in (xs, ys)
            ))
            if last:
                total = jnp.where(same, total + gram[u], 0.0)
                rowed[u] = jnp.sum(total.reshape(2 * ops, 16, 256), axis=1)
            else:
                gram[u] = total

    sinks = (
        (), ("sib",), flips + ("sib_flip",), ("next",), ("sib_next",), prevs, ("sib_prev",),
        ("half",), ("sib_half",),
    )
    products = {
        "Yx1": (x, yhi, ()),
        "Yx2": (x, yoh, partners),
        "Yb1": (xb, yhi, ("fore_tail", "fore_fifth", "fore_head")),
        "Yf1": (xf, yhi, ("back_tail", "back_fifth", "back_head")),
        "Yo1": (xo, yhi, ("pass_tail", "pass_fifth", "pass_head")),
        "Yb2": (xb, yoh, ("fore_pair", "fore_triple", "cross_b")),
        "Yf2": (xf, yoh, ("back_pair", "back_triple", "cross_f")),
        "Yo2": (xo, yoh, ("pass_pair", "pass_triple", "cross_o")),
    }
    begun = set()
    for name in ORDER:
        if name in sends:
            send(name)
        elif name == "half_own":
            send_half(jnp.logical_not(low), mine())
        elif name == "half_flip":
            arrive(flips)
            send_half(low, slot(FLIP))
        elif name in products:
            px, pyh, needs = products[name]
            arrive(needs)
            source_product(px, pyh, name[1] not in begun)
            begun.add(name[1])
        elif name[0] == "S":
            if name == "S0":
                own_load.wait()
                for u in range(UNITS):
                    prepare(u)
            u = int(name[1])
            arrive(sinks[u])
            sink_product(u)
        elif name == "T1":
            trace((x, xf, xb), False)
        else:
            trace((xo,), True)

    parts[...] = jnp.zeros_like(parts)
    pick_row = lax.broadcasted_iota(jnp.int32, (16, 256), 0)
    pick_group = lax.broadcasted_iota(jnp.int32, (16, 256), 1) // 16
    straight = jnp.where(pick_row == pick_group, 1.0, 0.0)
    crossed = jnp.where(
        pick_row < 8,
        jnp.where(pick_group == pick_row + 8, -1.0, 0.0),
        jnp.where(pick_group == pick_row - 8, 1.0, 0.0),
    )
    traces = exact_nt(rowed[:, 0:8].reshape(UNITS * 8, 256), straight) + exact_nt(
        rowed[:, 8:16].reshape(UNITS * 8, 256), crossed
    )
    for u in range(UNITS):
        parts[taus[u], cores[u], :, 0:16] = traces[8 * u : 8 * u + 8]

    part_copies = []
    for step in range(1, 8):
        to = lax.rem(snk + step, 8)
        copy = pltpu.make_async_remote_copy(
            src_ref=parts.at[to], dst_ref=sums.at[step], send_sem=part_send.at[step],
            recv_sem=part_recv.at[step], device_id=(src, to), device_id_type=MESH,
        )
        copy.start()
        part_copies.append(copy)
    sums[0] = parts[snk]
    for copy in part_copies:
        copy.wait()
    sums[0] = jnp.sum(sums[...], axis=0)
    def swap_copy(c):
        return pltpu.make_async_remote_copy(
            src_ref=sums.at[0, c], dst_ref=swapped.at[core], send_sem=swap_send.at[c],
            recv_sem=swap_recv.at[core], device_id=(snk * 2 + c, tau), device_id_type=MESH,
        )

    @pl.when(outside)
    def _():
        for c in range(2):
            swap_copy(c).start()
        for c in range(2):
            swap_copy(c).wait_send()
            pltpu.make_async_remote_copy(
                src_ref=sums.at[0, c], dst_ref=swapped.at[c], send_sem=swap_send.at[c],
                recv_sem=swap_recv.at[c], device_id=(snk * 2 + c, tau), device_id_type=MESH,
            ).wait_recv()

    turn_row = lax.broadcasted_iota(jnp.int32, (8, 128), 0)
    turn_lane = lax.broadcasted_iota(jnp.int32, (8, 128), 1)
    for c in range(2):
        for part in range(2):
            turn = jnp.where(turn_lane == turn_row + 8 * part, 1.0, 0.0)
            out[part, 0, c] = sums[0, c, :, 8 * part : 8 * part + 8] + exact_nt(turn, swapped[c])
    for name, (_, source, target, device, _) in sends.items():
        descriptor(name, source, target, device).wait_send()


def on_device(perambulators, elements):
    ops, rows, width = elements.shape[1], elements.shape[3], elements.shape[4]
    bf16, f32 = jnp.bfloat16, jnp.float32
    copies = 48
    return pl.pallas_call(
        kernel,
        out_shape=jax.ShapeDtypeStruct((2, 1, 2, ops, ops), f32),
        in_specs=[pl.BlockSpec(memory_space=pl.ANY)] * 2,
        out_specs=pl.BlockSpec(memory_space=pltpu.VMEM),
        scratch_shapes=[
            pltpu.VMEM((ops, 2, width, width), bf16),
            pltpu.VMEM((9, ops, 2, rows, width), bf16),
            pltpu.VMEM((UNITS, 2, width, width), bf16),
            pltpu.VMEM((2, UNITS, 2, rows, width), bf16),
            pltpu.VMEM((UNITS, 2, ops, rows, width), bf16),
            pltpu.VMEM((UNITS, 2, ops, rows, width), bf16),
            pltpu.VMEM((UNITS, 256, 256), f32),
            pltpu.VMEM((UNITS, 16, 256), f32),
            pltpu.VMEM((8, 2, 8, 128), f32),
            pltpu.VMEM((8, 2, 8, 128), f32),
            pltpu.VMEM((2, 8, 128), f32),
            pltpu.SemaphoreType.DMA((UNITS + 1,)),
            pltpu.SemaphoreType.DMA((copies,)),
            pltpu.SemaphoreType.DMA((copies,)),
            pltpu.SemaphoreType.DMA((8,)),
            pltpu.SemaphoreType.DMA((8,)),
            pltpu.SemaphoreType.DMA((2,)),
            pltpu.SemaphoreType.DMA((2,)),
        ],
        compiler_params=pltpu.CompilerParams(
            collective_id=0, has_side_effects=True, vmem_limit_bytes=62 * 2**20
        ),
        cost_estimate=pl.CostEstimate(
            flops=20 * 10**9, bytes_accessed=12 * 2**20, transcendentals=0
        ),
        name="correlate",
    )(perambulators, elements)


def solution(mesh):
    placed = (P("src", None, None, None, None), P("src", None, None, "snk", None))
    return jax.shard_map(
        on_device,
        mesh=mesh,
        in_specs=placed,
        out_specs=P(None, "src", "snk", None, None),
        check_vma=False,
    )
```

time: 102 us -> 97.4 us (0.955)
  Pallas kernels: 98.6 us -> 94.1 us
    pallas_call x1, Pallas kernels: 98.6 us -> 94.1 us  [on_device(): pl.pallas_call(kernel, out_shape=jax.ShapeDtypeStruct((2, 1, 2, ops, ops)...]
where the time goes in v3:
time: 97.4 us; the launch traced here: 95.5 us
  Pallas kernels  94.1 us (97%)
  local copies, waits for them, and re-layouts  1.32 us (1%)
    pallas_call x1, Pallas kernels, on_device(): pl.pallas_call(kernel, out_shape=jax.ShapeDtypeStruct((2, 1, 2, ops, ops)...  94.1 us

profile of v3, /device:TPU:11, one launch (start us, length us, event | category | flops | bytes accessed | tf_op | source)
XLA Modules:
  0.0 95.5 jit_solution(15342344446028987159)
XLA Ops:
  0.0 94.1 %correlate.1 = f32[2,1,2,8,8]{4,3,2,1,0:T(8,128)} custom-call(bf16[1,16,2,512,512]{4,3,2,1,0:T(8,128)(2,1)} %peram.1, bf16[1,8,2,64,512]{4,3,2,1,0:T(8,128)(2,1)} %elem.1), custom_call_target="tpu_custom_call" | custom-call | flops 20000000000 | bytes 12582912 | tf_op jit(solution)/shard_map/correlate/pallas_call | solution.py:415
  94.2 1.3 %copy.4 = f32[2,1,2,8,8]{4,3,2,1,0:T(8,128)} copy(f32[2,1,2,8,8]{4,3,2,1,0:T(8,128)} %correlate.1) | data formatting | bytes 2048

commit v4 on v3

--- a/solution.py
+++ b/solution.py
@@ -15,12 +15,12 @@
 
 ORDER = (
     "flip0", "flip1", "flip2", "flip3", "fore_tail", "back_tail", "fore_fifth", "back_fifth",
-    "fore_head", "back_head", "next", "half_own", "sib", "S0", "Yx1", "S1", "pass_fifth",
-    "yo0", "prev0", "yo1", "prev1", "yo2", "prev2", "yo3", "prev3", "half_flip", "sib_flip",
-    "S2", "cross_b", "pass_tail", "cross_f", "fore_pair", "back_pair", "Yb1", "pass_head",
-    "back_triple", "fore_triple", "Yx2", "Yf1", "sib_next", "S3", "sib_prev", "S5", "S4",
-    "pass_pair", "S6", "cross_o", "sib_half", "S7", "pass_triple", "Yb2", "S8", "Yo1",
-    "Yf2", "T1", "Yo2", "T2",
+    "fore_head", "back_head", "next", "sib", "S0", "yo0", "prev0", "yo1", "prev1", "yo2",
+    "prev2", "pass_tail", "cross_b", "cross_f", "yo3", "prev3", "half_own", "half_flip",
+    "pass_fifth", "Yx1", "sib_flip", "fore_pair", "back_pair", "S1", "S2", "back_triple",
+    "fore_triple", "pass_head", "Yb1", "sib_next", "Yf1", "S3", "S4", "cross_o", "cross_o5",
+    "pass_pair", "pass_twin", "Yx2", "Yf2", "sib_prev", "S5", "S6", "sib_half", "Yb2", "Yo1",
+    "S7", "T1a", "S8", "T1b", "Yo2", "T2",
 )
 
 
@@ -128,18 +128,23 @@
         )
     for target in (dev_flip, dev_flip_back, dev_zn, dev_zp, dev_zo, dev_sib):
         pl.semaphore_signal(barrier, inc=1, device_id=target, device_id_type=MESH)
-    outside = snk != tau
-
-    @pl.when(outside)
-    def _():
-        for c in range(2):
-            pl.semaphore_signal(barrier, inc=1, device_id=(snk * 2 + c, tau), device_id_type=MESH)
-
-    pl.semaphore_wait(barrier, jnp.where(outside, 15, 13))
+    def computed(c):
+        whole = (snk == tau) | (snk == next_tau) | (snk == prev_tau) | (snk == half_tau)
+        return whole | ((snk == flip_tau) & (flip_core == c))
+
+    for c in range(2):
+        @pl.when(jnp.logical_not(computed(c)))
+        def _(c=c):
+            for k in range(8):
+                pl.semaphore_signal(
+                    barrier, inc=1, device_id=(snk * 2 + c, k), device_id_type=MESH
+                )
+
+    pl.semaphore_wait(barrier, 13 + UNITS - 2)
 
     quarters = ((0, 2), (2, 2), (4, 2), (6, 2))
     tail, fifth, head = (5, 3), (4, 1), (0, 4)
-    pair, triple = (0, 2), (2, 3)
+    pair, triple, twin = (0, 2), (2, 3), (2, 2)
 
     def block(px, pyh, piece):
         start = pl.multiple_of((px * 2 + pyh) * rows, rows)
@@ -182,15 +187,19 @@
         ("fifth", "fore_", xb, yhi, fifth, dev_fore),
         ("head", "back_", xf, yhi, head, dev_back),
         ("pair", "fore_", xb, yoh, pair, dev_fore),
-        ("triple", "back_", xf, yoh, triple, dev_back),
+        ("twin", "back_", xf, yoh, twin, dev_back),
     ):
         here = block(px, pyh, piece)
-        sends["pass_" + name] = ((side + name,), here, here, device, block(xo, pyh, piece))
-    for name, needs, px in (
-        ("cross_b", "fore_tail", xb), ("cross_f", "back_tail", xf), ("cross_o", "pass_tail", xo)
+        source = "triple" if piece is twin else name
+        sends["pass_" + name] = ((side + source,), here, here, device, block(xo, pyh, piece))
+    for name, needs, px, piece in (
+        ("cross_b", "fore_tail", xb, tail),
+        ("cross_f", "back_tail", xf, tail),
+        ("cross_o", "pass_tail", xo, tail),
+        ("cross_o5", "pass_fifth", xo, fifth),
     ):
-        here = block(px, yhi, tail)
-        sends[name] = ((needs,), here, here, dev_yo, block(px, yoh, tail))
+        here = block(px, yhi, piece)
+        sends[name] = ((needs,), here, here, dev_yo, block(px, yoh, piece))
     sends["next"] = ((), mine(), slot(NEXT), dev_zp, slot(NEXT))
     sends["half"] = ((), mine(), slot(HALF), dev_zo, slot(HALF))
     for name, needs, source, target in (
@@ -292,8 +301,8 @@
     c_iota = lax.broadcasted_iota(jnp.int32, (256, 256), 1)
     same = lax.rem(r_iota, 16) == lax.rem(c_iota, 16)
 
-    def trace(columns, last):
-        for u in range(UNITS):
+    def trace(columns, units, last):
+        for u in units:
             total = dot_nt(*(
                 jnp.concatenate(
                     [
@@ -324,7 +333,7 @@
         "Yo1": (xo, yhi, ("pass_tail", "pass_fifth", "pass_head")),
         "Yb2": (xb, yoh, ("fore_pair", "fore_triple", "cross_b")),
         "Yf2": (xf, yoh, ("back_pair", "back_triple", "cross_f")),
-        "Yo2": (xo, yoh, ("pass_pair", "pass_triple", "cross_o")),
+        "Yo2": (xo, yoh, ("pass_pair", "pass_twin", "cross_o", "cross_o5")),
     }
     begun = set()
     for name in ORDER:
@@ -348,10 +357,12 @@
             u = int(name[1])
             arrive(sinks[u])
             sink_product(u)
-        elif name == "T1":
-            trace((x, xf, xb), False)
+        elif name == "T1a":
+            trace((x, xf, xb), range(7), False)
+        elif name == "T1b":
+            trace((x, xf, xb), range(7, UNITS), False)
         else:
-            trace((xo,), True)
+            trace((xo,), range(UNITS), True)
 
     parts[...] = jnp.zeros_like(parts)
     pick_row = lax.broadcasted_iota(jnp.int32, (16, 256), 0)
@@ -368,6 +379,15 @@
     for u in range(UNITS):
         parts[taus[u], cores[u], :, 0:16] = traces[8 * u : 8 * u + 8]
 
+    swap_copies = []
+    for u in range(2, UNITS):
+        copy = pltpu.make_async_remote_copy(
+            src_ref=parts.at[taus[u], cores[u]], dst_ref=swapped.at[core, snk],
+            send_sem=swap_send.at[u - 2], recv_sem=swap_recv.at[core, snk],
+            device_id=(taus[u] * 2 + cores[u], tau), device_id_type=MESH,
+        )
+        copy.start()
+        swap_copies.append(copy)
     part_copies = []
     for step in range(1, 8):
         to = lax.rem(snk + step, 8)
@@ -380,30 +400,26 @@
     sums[0] = parts[snk]
     for copy in part_copies:
         copy.wait()
-    sums[0] = jnp.sum(sums[...], axis=0)
-    def swap_copy(c):
-        return pltpu.make_async_remote_copy(
-            src_ref=sums.at[0, c], dst_ref=swapped.at[core], send_sem=swap_send.at[c],
-            recv_sem=swap_recv.at[core], device_id=(snk * 2 + c, tau), device_id_type=MESH,
-        )
-
-    @pl.when(outside)
-    def _():
-        for c in range(2):
-            swap_copy(c).start()
-        for c in range(2):
-            swap_copy(c).wait_send()
-            pltpu.make_async_remote_copy(
-                src_ref=sums.at[0, c], dst_ref=swapped.at[c], send_sem=swap_send.at[c],
-                recv_sem=swap_recv.at[c], device_id=(snk * 2 + c, tau), device_id_type=MESH,
-            ).wait_recv()
+    for c in range(2):
+        @pl.when(jnp.logical_not(computed(c)))
+        def _(c=c):
+            for k in range(8):
+                pltpu.make_async_remote_copy(
+                    src_ref=swapped.at[c, k], dst_ref=swapped.at[c, k],
+                    send_sem=swap_send.at[0], recv_sem=swap_recv.at[c, k],
+                    device_id=dev_sib, device_id_type=MESH,
+                ).wait_recv()
+    for copy in swap_copies:
+        copy.wait_send()
 
     turn_row = lax.broadcasted_iota(jnp.int32, (8, 128), 0)
     turn_lane = lax.broadcasted_iota(jnp.int32, (8, 128), 1)
     for c in range(2):
+        total = jnp.sum(sums[:, c], axis=0)
+        other_total = jnp.sum(swapped[c], axis=0)
         for part in range(2):
             turn = jnp.where(turn_lane == turn_row + 8 * part, 1.0, 0.0)
-            out[part, 0, c] = sums[0, c, :, 8 * part : 8 * part + 8] + exact_nt(turn, swapped[c])
+            out[part, 0, c] = total[:, 8 * part : 8 * part + 8] + exact_nt(turn, other_total)
     for name, (_, source, target, device, _) in sends.items():
         descriptor(name, source, target, device).wait_send()
 
@@ -428,14 +444,14 @@
             pltpu.VMEM((UNITS, 16, 256), f32),
             pltpu.VMEM((8, 2, 8, 128), f32),
             pltpu.VMEM((8, 2, 8, 128), f32),
-            pltpu.VMEM((2, 8, 128), f32),
+            pltpu.VMEM((2, 8, 8, 128), f32),
             pltpu.SemaphoreType.DMA((UNITS + 1,)),
             pltpu.SemaphoreType.DMA((copies,)),
             pltpu.SemaphoreType.DMA((copies,)),
             pltpu.SemaphoreType.DMA((8,)),
             pltpu.SemaphoreType.DMA((8,)),
-            pltpu.SemaphoreType.DMA((2,)),
-            pltpu.SemaphoreType.DMA((2,)),
+            pltpu.SemaphoreType.DMA((UNITS - 2,)),
+            pltpu.SemaphoreType.DMA((2, 8)),
         ],
         compiler_params=pltpu.CompilerParams(
             collective_id=0, has_side_effects=True, vmem_limit_bytes=62 * 2**20

time: 97.4 us -> 87.4 us (0.90); the launches traced: 95.5 us -> 87.2 us
  Pallas kernels: 94.1 us -> 85.9 us
    pallas_call x1, Pallas kernels: 94.1 us -> 85.9 us  [on_device(): pl.pallas_call(kernel, out_shape=jax.ShapeDtypeStruct((2, 1, 2, ops, ops)...]
where the time goes in v4:
time: 87.4 us; the launch traced here: 87.2 us
  Pallas kernels  85.9 us (98%)
  local copies, waits for them, and re-layouts  1.32 us (2%)
    pallas_call x1, Pallas kernels, on_device(): pl.pallas_call(kernel, out_shape=jax.ShapeDtypeStruct((2, 1, 2, ops, ops)...  85.9 us

profile of v4, /device:TPU:11, one launch (start us, length us, event | category | flops | bytes accessed | tf_op | source)
XLA Modules:
  0.0 87.2 jit_solution(3945508902205131498)
XLA Ops:
  0.0 85.9 %correlate.1 = f32[2,1,2,8,8]{4,3,2,1,0:T(8,128)} custom-call(bf16[1,16,2,512,512]{4,3,2,1,0:T(8,128)(2,1)} %peram.1, bf16[1,8,2,64,512]{4,3,2,1,0:T(8,128)(2,1)} %elem.1), custom_call_target="tpu_custom_call" | custom-call | flops 20000000000 | bytes 12582912 | tf_op jit(solution)/shard_map/correlate/pallas_call | solution.py:431
  85.9 1.3 %copy.4 = f32[2,1,2,8,8]{4,3,2,1,0:T(8,128)} copy(f32[2,1,2,8,8]{4,3,2,1,0:T(8,128)} %correlate.1) | data formatting | bytes 2048

commit v5 on v4

--- a/solution.py
+++ b/solution.py
@@ -16,11 +16,11 @@
 ORDER = (
     "flip0", "flip1", "flip2", "flip3", "fore_tail", "back_tail", "fore_fifth", "back_fifth",
     "fore_head", "back_head", "next", "sib", "S0", "yo0", "prev0", "yo1", "prev1", "yo2",
-    "prev2", "pass_tail", "cross_b", "cross_f", "yo3", "prev3", "half_own", "half_flip",
-    "pass_fifth", "Yx1", "sib_flip", "fore_pair", "back_pair", "S1", "S2", "back_triple",
-    "fore_triple", "pass_head", "Yb1", "sib_next", "Yf1", "S3", "S4", "cross_o", "cross_o5",
-    "pass_pair", "pass_twin", "Yx2", "Yf2", "sib_prev", "S5", "S6", "sib_half", "Yb2", "Yo1",
-    "S7", "T1a", "S8", "T1b", "Yo2", "T2",
+    "prev2", "pass_tail", "cross_b", "cross_f", "yo3", "prev3", "pass_fifth", "Yx1", "sib_flip",
+    "fore_pair", "back_pair", "S1", "S2", "back_triple", "fore_triple", "pass_head", "Yb1",
+    "sib_next", "half_own", "half_flip", "Yf1", "S3", "S4", "cross_o", "cross_o5", "pass_pair",
+    "pass_twin", "sib_prev", "S5", "S6", "Yx2", "Yf2l", "Yf2u", "T1a", "Yb2u", "Yb2l", "Yo1",
+    "sib_half", "S7", "S8", "T1b", "Yo2u", "Yo2l", "T2",
 )
 
 
@@ -108,6 +108,27 @@
         FLIP_PREV, SIB_FLIP_PREV, HALF, SIB_HALF,
     ]
 
+    swapped[...] = jnp.zeros_like(swapped)
+
+    barrier = pltpu.get_barrier_semaphore()
+    for step in range(1, 8):
+        pl.semaphore_signal(
+            barrier, inc=1, device_id=(src, lax.rem(snk + step, 8)), device_id_type=MESH
+        )
+    for target in (dev_flip, dev_flip_back, dev_zn, dev_zp, dev_zo, dev_sib):
+        pl.semaphore_signal(barrier, inc=1, device_id=target, device_id_type=MESH)
+    def computed(c):
+        whole = (snk == tau) | (snk == next_tau) | (snk == prev_tau) | (snk == half_tau)
+        return whole | ((snk == flip_tau) & (flip_core == c))
+
+    for c in range(2):
+        @pl.when(jnp.logical_not(computed(c)))
+        def _(c=c):
+            for k in range(8):
+                pl.semaphore_signal(
+                    barrier, inc=1, device_id=(snk * 2 + c, k), device_id_type=MESH
+                )
+
     own_slice = full.at[:, :, pl.ds(pl.multiple_of(snk * rows, rows), rows), :]
     own_load = pltpu.make_async_copy(elem.at[0], own_slice, load_sem.at[UNITS])
     own_load.start()
@@ -118,27 +139,6 @@
         )
         load.start()
         loads.append(load)
-
-    swapped[...] = jnp.zeros_like(swapped)
-
-    barrier = pltpu.get_barrier_semaphore()
-    for step in range(1, 8):
-        pl.semaphore_signal(
-            barrier, inc=1, device_id=(src, lax.rem(snk + step, 8)), device_id_type=MESH
-        )
-    for target in (dev_flip, dev_flip_back, dev_zn, dev_zp, dev_zo, dev_sib):
-        pl.semaphore_signal(barrier, inc=1, device_id=target, device_id_type=MESH)
-    def computed(c):
-        whole = (snk == tau) | (snk == next_tau) | (snk == prev_tau) | (snk == half_tau)
-        return whole | ((snk == flip_tau) & (flip_core == c))
-
-    for c in range(2):
-        @pl.when(jnp.logical_not(computed(c)))
-        def _(c=c):
-            for k in range(8):
-                pl.semaphore_signal(
-                    barrier, inc=1, device_id=(snk * 2 + c, k), device_id_type=MESH
-                )
 
     pl.semaphore_wait(barrier, 13 + UNITS - 2)
 
@@ -270,7 +270,7 @@
 
     lane = lax.broadcasted_iota(jnp.int32, (384, 128), 1)
 
-    def source_product(px, pyh, first):
+    def source_product(px, pyh, first, groups):
         cols = pl.ds(pl.multiple_of(px * 128, 128), 128)
         krows = pl.ds(pl.multiple_of((px * 2 + pyh) * rows, rows), rows)
         here = (lane // 64) == pyh
@@ -279,7 +279,7 @@
             a = jnp.concatenate(
                 [left[0, units].reshape(384, 512), left[1, units].reshape(384, 512)], axis=1
             )
-            for q in range(ops // 4):
+            for q in groups:
                 w = jnp.concatenate(
                     [full[4 * q : 4 * q + 4, c, krows, :].reshape(256, 512) for c in range(2)],
                     axis=1,
@@ -325,17 +325,20 @@
         (), ("sib",), flips + ("sib_flip",), ("next",), ("sib_next",), prevs, ("sib_prev",),
         ("half",), ("sib_half",),
     )
+    both = (0, 1)
     products = {
-        "Yx1": (x, yhi, ()),
-        "Yx2": (x, yoh, partners),
-        "Yb1": (xb, yhi, ("fore_tail", "fore_fifth", "fore_head")),
-        "Yf1": (xf, yhi, ("back_tail", "back_fifth", "back_head")),
-        "Yo1": (xo, yhi, ("pass_tail", "pass_fifth", "pass_head")),
-        "Yb2": (xb, yoh, ("fore_pair", "fore_triple", "cross_b")),
-        "Yf2": (xf, yoh, ("back_pair", "back_triple", "cross_f")),
-        "Yo2": (xo, yoh, ("pass_pair", "pass_twin", "cross_o", "cross_o5")),
+        "Yx1": (x, yhi, both, ()),
+        "Yx2": (x, yoh, both, partners),
+        "Yb1": (xb, yhi, both, ("fore_tail", "fore_fifth", "fore_head")),
+        "Yf1": (xf, yhi, both, ("back_tail", "back_fifth", "back_head")),
+        "Yo1": (xo, yhi, both, ("pass_tail", "pass_fifth", "pass_head")),
+        "Yb2u": (xb, yoh, (1,), ("fore_triple", "cross_b")),
+        "Yb2l": (xb, yoh, (0,), ("fore_pair", "fore_triple")),
+        "Yf2u": (xf, yoh, (1,), ("back_triple", "cross_f")),
+        "Yf2l": (xf, yoh, (0,), ("back_pair", "back_triple")),
+        "Yo2u": (xo, yoh, (1,), ("cross_o", "cross_o5")),
+        "Yo2l": (xo, yoh, (0,), ("pass_pair", "pass_twin")),
     }
-    begun = set()
     for name in ORDER:
         if name in sends:
             send(name)
@@ -345,10 +348,9 @@
             arrive(flips)
             send_half(low, slot(FLIP))
         elif name in products:
-            px, pyh, needs = products[name]
+            px, pyh, groups, needs = products[name]
             arrive(needs)
-            source_product(px, pyh, name[1] not in begun)
-            begun.add(name[1])
+            source_product(px, pyh, name[2] == "1", groups)
         elif name[0] == "S":
             if name == "S0":
                 own_load.wait()
@@ -358,11 +360,11 @@
             arrive(sinks[u])
             sink_product(u)
         elif name == "T1a":
-            trace((x, xf, xb), range(7), False)
+            trace((x, xf), range(7), False)
         elif name == "T1b":
-            trace((x, xf, xb), range(7, UNITS), False)
+            trace((x, xf), range(7, UNITS), False)
         else:
-            trace((xo,), range(UNITS), True)
+            trace((xb, xo), range(UNITS), True)
 
     parts[...] = jnp.zeros_like(parts)
     pick_row = lax.broadcasted_iota(jnp.int32, (16, 256), 0)

time: 87.4 us -> 86.1 us (0.985)
  Pallas kernels: 85.9 us -> 84.6 us
    pallas_call x1, Pallas kernels: 85.9 us -> 84.6 us  [on_device(): pl.pallas_call(kernel, out_shape=jax.ShapeDtypeStruct((2, 1, 2, ops, ops)...]
where the time goes in v5:
time: 86.1 us; the launch traced here: 85.9 us
  Pallas kernels  84.6 us (98%)
  local copies, waits for them, and re-layouts  1.32 us (2%)
    pallas_call x1, Pallas kernels, on_device(): pl.pallas_call(kernel, out_shape=jax.ShapeDtypeStruct((2, 1, 2, ops, ops)...  84.6 us

profile of v5, /device:TPU:11, one launch (start us, length us, event | category | flops | bytes accessed | tf_op | source)
XLA Modules:
  0.0 85.9 jit_solution(6812081688157783730)
XLA Ops:
  0.0 84.6 %correlate.1 = f32[2,1,2,8,8]{4,3,2,1,0:T(8,128)} custom-call(bf16[1,16,2,512,512]{4,3,2,1,0:T(8,128)(2,1)} %peram.1, bf16[1,8,2,64,512]{4,3,2,1,0:T(8,128)(2,1)} %elem.1), custom_call_target="tpu_custom_call" | custom-call | flops 20000000000 | bytes 12582912 | tf_op jit(solution)/shard_map/correlate/pallas_call | solution.py:433
  84.6 1.3 %copy.4 = f32[2,1,2,8,8]{4,3,2,1,0:T(8,128)} copy(f32[2,1,2,8,8]{4,3,2,1,0:T(8,128)} %correlate.1) | data formatting | bytes 2048

commit v6 on v5

--- a/solution.py
+++ b/solution.py
@@ -18,9 +18,9 @@
     "fore_head", "back_head", "next", "sib", "S0", "yo0", "prev0", "yo1", "prev1", "yo2",
     "prev2", "pass_tail", "cross_b", "cross_f", "yo3", "prev3", "pass_fifth", "Yx1", "sib_flip",
     "fore_pair", "back_pair", "S1", "S2", "back_triple", "fore_triple", "pass_head", "Yb1",
-    "sib_next", "half_own", "half_flip", "Yf1", "S3", "S4", "cross_o", "cross_o5", "pass_pair",
-    "pass_twin", "sib_prev", "S5", "S6", "Yx2", "Yf2l", "Yf2u", "T1a", "Yb2u", "Yb2l", "Yo1",
-    "sib_half", "S7", "S8", "T1b", "Yo2u", "Yo2l", "T2",
+    "sib_next", "half_own", "half_flip", "Yf1", "S3", "S4", "cross_o", "sib_prev", "S5",
+    "cross_o5", "S6", "pass_pair", "pass_twin", "Yx2", "Yf2l", "Yf2u", "T1a", "Yb2u",
+    "sib_half", "Yb2l", "S7", "S8", "Yo1", "T1b", "Yo2u", "Yo2l", "T2",
 )
 
 

time: 86.1 us -> 86.3 us (level)
  no operation moved by 1% of the time
where the time goes in v6:
time: 86.3 us; the launch traced here: 85.7 us
  Pallas kernels  84.4 us (98%)
  local copies, waits for them, and re-layouts  1.32 us (2%)
    pallas_call x1, Pallas kernels, on_device(): pl.pallas_call(kernel, out_shape=jax.ShapeDtypeStruct((2, 1, 2, ops, ops)...  84.4 us

profile of v6, /device:TPU:11, one launch (start us, length us, event | category | flops | bytes accessed | tf_op | source)
XLA Modules:
  0.0 85.7 jit_solution(8890374586309758165)
XLA Ops:
  0.0 84.4 %correlate.1 = f32[2,1,2,8,8]{4,3,2,1,0:T(8,128)} custom-call(bf16[1,16,2,512,512]{4,3,2,1,0:T(8,128)(2,1)} %peram.1, bf16[1,8,2,64,512]{4,3,2,1,0:T(8,128)(2,1)} %elem.1), custom_call_target="tpu_custom_call" | custom-call | flops 20000000000 | bytes 12582912 | tf_op jit(solution)/shard_map/correlate/pallas_call | solution.py:433
  84.4 1.3 %copy.4 = f32[2,1,2,8,8]{4,3,2,1,0:T(8,128)} copy(f32[2,1,2,8,8]{4,3,2,1,0:T(8,128)} %correlate.1) | data formatting | bytes 2048
